TPU v7x, 32 devices: a whole 2x2x4 slice. The times are simulated.
32 devices in a mesh: row: 4 (over y, x), col: 8 (over z, core).
Axes of the slice: x: 2, y: 2, z: 4, core: 2. Of those that a mesh axis runs over, the one named last changes fastest.
Arguments:
- omega_sq: float32 [8192, 8192], P('row', 'col'), may hold values from -6 to 6
- pole_freq: float32 [8192, 8192], P('row', 'col'), may hold values from 0.5 to 4
- mtx_left: float32 [1, 8192, 128], P(None, ('row', 'col')), may hold values from -0.0625 to 0.0625
- mtx_right: float32 [1, 8192, 128], P(None, ('col', 'row')), may hold values from -0.0625 to 0.0625
- band_ids: int32 [1], replicated, may hold values from 0 to 63
- band_energy: float32 [64], replicated, may hold values from -3 to 1
- eval_energy: float32 [3], replicated, may hold values from -1 to 1
Outputs:
- sigma: float32 [128, 384], replicated
All inputs are finite; a program needn't handle non-finite values.
Results may differ from a plain program's by a relative error of at most 0.0001.
Values sent between devices are 32-bit elements; how exact they have to be, the bound alone decides.
A program may use at most 64 MiB of HBM per device.

v0:
```python
import jax
import jax.numpy as jnp
from jax import lax
from jax.sharding import PartitionSpec as P


def contract_rows(left, right):
    return lax.dot_general(
        left,
        right,
        (((0,), (0,)), ((), ())),
        precision=lax.Precision.HIGHEST,
        preferred_element_type=jnp.float32,
    )


def kernel_rows(ratio, freq, shift_row, right_cols, energies):
    parts = []
    for energy in range(energies):
        gap = shift_row[energy] - freq
        kern = ratio * gap / (gap * gap + 0.09)
        parts.append(
            jnp.dot(
                kern,
                right_cols,
                preferred_element_type=jnp.float32,
                precision=lax.Precision.HIGHEST,
            )
        )
    return jnp.concatenate(parts, axis=1)


def shards(omega_sq, pole_freq, mtx_left, mtx_right, band_ids, band_energy, eval_energy):
    table = band_energy.shape[0]
    energies = eval_energy.shape[0]
    hits = (band_ids[:, None] == jnp.arange(table, dtype=jnp.int32)[None, :]).astype(jnp.float32)
    levels = jnp.sum(hits * band_energy[None, :], axis=1)
    shifts = eval_energy[None, :] - levels[:, None]
    ratio = omega_sq / pole_freq
    shift_row = shifts[0]
    right_cols = lax.all_gather(mtx_right[0], "row", axis=0, tiled=True)
    product = kernel_rows(ratio, pole_freq, shift_row, right_cols, energies)
    total = contract_rows(lax.all_gather(mtx_left[0], "col", axis=0, tiled=True), product)
    return lax.psum(total, ("row", "col"))


def solution(mesh):
    return jax.shard_map(
        shards,
        mesh=mesh,
        in_specs=(
            P("row", "col"),
            P("row", "col"),
            P(None, ("row", "col"), None),
            P(None, ("col", "row"), None),
            P(),
            P(),
            P(),
        ),
        out_specs=P(),
        check_vma=False,
    )
```

profile of v0, /device:TPU:0, one launch (start us, length us, event | category | flops | bytes accessed | tf_op | source)
XLA Modules:
  0.0 194.0 jit_solution(843797200771383153)
XLA Ops:
  6.5 0.0 all-gather.4.cloned.1.call-start
  6.5 0.7 all-gather.4.cloned.1.call-update
  7.3 0.0 all-reduce.2.cloned.1.call-start
  7.3 0.0 slice-start
  7.3 0.0 slice-start.2
  7.3 12.8 %all-gather = f32[1,1024,128]{2,1,0:T(8,128)S(1)} all-gather(f32[1,256,128]{2,1,0:T(8,128)} %param.10), channel_id=2, replica_groups=mesh['row'=4,'col'=8] {'row'}, dimensions={1}, use_global_device_ids=true | all-gather | bytes 655360 | tf_op jit(solution)/shard_map/all_gather | solution.py:41
  20.8 1.3 fusion.22
  22.1 1.3 subtract_bitcast_fusion
  23.3 0.6 fusion.30
  24.0 0.0 slice-start.1
  24.0 0.0 slice-start.3
  24.0 12.9 %fusion = f32[2048,128]{1,0:T(8,128)S(1)} fusion(f32[2048,1024]{1,0:T(8,128)} %param.8, f32[]{:T(128)} %bitcast.2, f32[1,1024,128]{2,1,0:T(8,128)S(1)} %all-gather, f32[2048,1024]{1,0:T(8,128)} %param.7), kind=kOutput, calls=%fused_computation.3 | convolution fusion | flops 3233808384 | bytes 18350084 | tf_op jit(solution)/shard_map/dot_general | solution.py:23
  36.8 0.0 slice-done
  36.8 0.0 slice-done.2
  36.9 0.0 slice-done.1
  36.9 0.0 slice-done.3
  36.9 8.9 %fusion.1 = f32[2048,128]{1,0:T(8,128)S(1)} fusion(f32[2048,1024]{1,0:T(8,128)S(1)} %bitcast.20, f32[]{:T(128)} %bitcast.4, f32[1,1024,128]{2,1,0:T(8,128)S(1)} %all-gather, f32[2048,1024]{1,0:T(8,128)S(1)} %bitcast.22), kind=kOutput, calls=%fused_computation.4 | convolution fusion | flops 3233808384 | bytes 18350084 | tf_op jit(solution)/shard_map/dot_general | solution.py:23
  45.8 9.1 %fusion.2 = f32[2048,128]{1,0:T(8,128)S(1)} fusion(f32[2048,1024]{1,0:T(8,128)S(1)} %bitcast.20, f32[]{:T(128)} %bitcast.5, f32[1,1024,128]{2,1,0:T(8,128)S(1)} %all-gather, f32[2048,1024]{1,0:T(8,128)S(1)} %bitcast.22), kind=kOutput, calls=%fused_computation.5 | convolution fusion | flops 3233808384 | bytes 18350084 | tf_op jit(solution)/shard_map/dot_general | solution.py:23
  54.9 0.0 all-gather.4.cloned.1.call-done
  55.0 6.9 %fusion.15 = f32[128,384]{0,1:T(8,128)} fusion(f32[2048,128]{1,0:T(8,128)S(1)} %fusion.2, f32[2048,128]{1,0:T(8,128)S(1)} %fusion.1, f32[2048,128]{1,0:T(8,128)S(1)} %fusion, f32[1,2048,128]{2,1,0:T(8,128)} %all-gather.4.cloned.1.call-done), kind=kOutput, calls=%fused_computation.18 | convolution fusion | flops 1209532416 | bytes 4390912 | tf_op jit(solution)/shard_map/dot_general | solution.py:8
  61.9 0.0 all-reduce.2.cloned.1.call-update
  61.9 123.5 %all-reduce.2.cloned.1.call-done = f32[128,384]{0,1:T(8,128)} async-done(((f32[128,384]{0,1:T(8,128)}), f32[128,384]{0,1:T(8,128)}) %all-reduce.2.cloned.1.call-update) | async-done | bytes 196624 | tf_op jit(solution)/shard_map/psum | solution.py:44
  185.4 1.7 copy.8
  (2 shorter events, 0.0 us)
Async XLA Ops:
  6.5 48.4 %all-gather.4.cloned.1.call-start = ((), (), s32[]{:S(2)}) async-start(), calls=%async_computation.1 | async-start | bytes 1179648 | tf_op jit(solution)/shard_map/all_gather | solution.py:43
  7.3 178.2 %all-reduce.2.cloned.1.call-start = ((), (), s32[]{:S(2)}) async-start(), calls=%async_computation | async-start | bytes 393216 | tf_op jit(solution)/shard_map/psum | solution.py:44
  7.3 29.5 %slice-start = ((s8[8388608]{0:T(1024)(128)(4,1)}), s8[4194304]{0:T(1024)(128)(4,1)S(1)}, s32[]{:S(2)}) async-start(s8[8388608]{0:T(1024)(128)(4,1)} %bitcast.19), calls=%async_computation.2 | async-start | bytes 8388608
  7.3 29.5 %slice-start.2 = ((s8[8388608]{0:T(1024)(128)(4,1)}), s8[4194304]{0:T(1024)(128)(4,1)S(1)}, s32[]{:S(2)}) async-start(s8[8388608]{0:T(1024)(128)(4,1)} %bitcast.21), calls=%async_computation.4 | async-start | bytes 8388608
  24.0 12.9 %slice-start.1 = ((s8[8388608]{0:T(1024)(128)(4,1)}), s8[4194304]{0:T(1024)(128)(4,1)S(1)}, s32[]{:S(2)}) async-start(s8[8388608]{0:T(1024)(128)(4,1)} %bitcast.19), calls=%async_computation.3 | async-start | bytes 8388608
  24.0 12.9 %slice-start.3 = ((s8[8388608]{0:T(1024)(128)(4,1)}), s8[4194304]{0:T(1024)(128)(4,1)S(1)}, s32[]{:S(2)}) async-start(s8[8388608]{0:T(1024)(128)(4,1)} %bitcast.21), calls=%async_computation.5 | async-start | bytes 8388608
Sparse Core Ops, SparseCore 0:
  9.0 24.7 all-gather.3
  62.1 123.3 all-reduce.1
where the time goes:
time: 195 us; the launch traced here: 194 us
  waiting for transfers between devices  124 us (64%)
  matrix products  37.8 us (19%)
  between operations  14.1 us (7%)
  blocking collectives  12.8 us (7%)
  other arithmetic  2.55 us (1%)
  local copies, waits for them, and re-layouts  2.37 us (1%)
    psum x1, waiting for transfers between devices, shards(): return lax.psum(total, ('row', 'col'))  123 us
    dot_general x3, matrix products, kernel_rows(): jnp.dot(kern, right_cols, preferred_element_type=jnp.float32, precision=l...  30.9 us
    all_gather x1, blocking collectives, shards(): right_cols = lax.all_gather(mtx_right[0], 'row', axis=0, tiled=True)  12.8 us
    dot_general x1, matrix products, contract_rows(): lax.dot_general(left, right, (((0,), (0,)), ((), ())), precision=lax.Prec...  6.94 us
  transfers between devices with their start and end apart: 2, of which 1 were waited for; matrix products, arithmetic and copies ran while one was open for 18% of the time, Pallas kernels for 0%

commit v1 on v0

v1 whole, which is shorter than its diff:
```python
import functools

import jax
import jax.numpy as jnp
from jax import lax
from jax.experimental import pallas as pl
from jax.experimental.pallas import tpu as pltpu
from jax.sharding import PartitionSpec as P

MESH = pl.DeviceIdType.MESH
F32 = jnp.float32
BF16 = jnp.bfloat16


def contract_rows(left, right):
    return lax.dot_general(
        left,
        right,
        (((0,), (0,)), ((), ())),
        precision=lax.Precision.HIGHEST,
        preferred_element_type=F32,
    )


def plain(omega_sq, pole_freq, mtx_left, mtx_right, band_ids, band_energy, eval_energy):
    shifts = eval_energy - band_energy[band_ids[0]]
    ratio = omega_sq / pole_freq
    right_cols = lax.all_gather(mtx_right[0], "row", axis=0, tiled=True)
    parts = []
    for energy in range(eval_energy.shape[0]):
        gap = shifts[energy] - pole_freq
        kern = ratio * gap / (gap * gap + 0.09)
        parts.append(jnp.dot(kern, right_cols, preferred_element_type=F32, precision=lax.Precision.HIGHEST))
    product = jnp.concatenate(parts, axis=1)
    total = contract_rows(lax.all_gather(mtx_left[0], "col", axis=0, tiled=True), product)
    return lax.psum(total, ("row", "col"))


def flip(value, mask):
    bit, out = 1, value
    while bit <= mask:
        if mask & bit:
            out = out + bit - 2 * bit * lax.rem(lax.div(value, bit), 2)
        bit *= 2
    return out


def split(x):
    high = x.astype(BF16)
    return high, (x - high.astype(F32)).astype(BF16)


def body(
    nrow, ncol, tile,
    ids, levels, evals, w_hbm, f_hbm, l_hbm, r_hbm, out,
    wbuf, fbuf, rbuf, lbuf, rsplit, acc, sigma, part, recv, gat,
    wsem, fsem, ownsem, rsend, rrecv, lsend, lrecv, ssend, srecv, gsend, grecv,
):
    ne = evals.shape[0]
    rows, depth = wbuf.shape[1:]
    lrows, ns = lbuf.shape[1:]
    n = nrow * ncol
    row, col = lax.axis_index("row"), lax.axis_index("col")
    me = row * ncol + col

    loads = []
    for s in range(nrow):
        cols = pl.ds(pl.multiple_of(flip(row, s) * depth, depth), depth)
        pair = [
            pltpu.make_async_copy(f_hbm.at[:, cols], fbuf.at[s], fsem.at[s]),
            pltpu.make_async_copy(w_hbm.at[:, cols], wbuf.at[s], wsem.at[s]),
        ]
        loads.append(pair)
    own = [
        pltpu.make_async_copy(r_hbm, rbuf.at[0], ownsem.at[0]),
        pltpu.make_async_copy(l_hbm, lbuf.at[0], ownsem.at[1]),
    ]

    barrier = pltpu.get_barrier_semaphore()

    @pl.loop(1, n)
    def _(d):
        peer = lax.rem(me + d, n)
        pl.semaphore_signal(barrier, inc=1, device_id=(lax.div(peer, ncol), lax.rem(peer, ncol)), device_id_type=MESH)

    own[0].start()
    for copy in loads[0]:
        copy.start()
    own[1].start()
    for pair in loads[1:]:
        for copy in pair:
            copy.start()
    pl.semaphore_wait(barrier, n - 1)

    rcopies = [None] + [
        pltpu.make_async_remote_copy(
            r_hbm, rbuf.at[s], rsend.at[s], rrecv.at[s],
            device_id=(flip(row, s), col), device_id_type=MESH,
        )
        for s in range(1, nrow)
    ]
    lcopies = [None] * ncol
    for d in range(1, ncol):
        direct = d == 1 or d % 2 == 0
        lcopies[d] = pltpu.make_async_remote_copy(
            l_hbm if direct else lbuf.at[d - 1], lbuf.at[d], lsend.at[d], lrecv.at[d],
            device_id=(row, flip(col, d if direct else 1)), device_id_type=MESH,
        )
    for copy in rcopies[1:]:
        copy.start()
    lcopies[1].start()
    for d in range(2, ncol, 2):
        lcopies[d].start()

    level = levels[ids[0]]
    shifts = [evals[k] - level for k in range(ne)]

    for s in range(nrow):
        if s == 0:
            own[0].wait()
        else:
            rcopies[s].wait_recv()
        high, low = split(rbuf[s])
        rsplit[:, :ns] = high
        rsplit[:, ns:] = low
        for copy in loads[s]:
            copy.wait()

        @pl.loop(0, rows // tile)
        def _(t):
            at = pl.ds(pl.multiple_of(t * tile, tile), tile)
            freq = fbuf[s, at, :]
            ratio = wbuf[s, at, :] * pltpu.reciprocal(freq, approx=True)
            both = rsplit[...]
            for k in range(ne):
                gap = shifts[k] - freq
                kern = ratio * gap * pltpu.reciprocal(gap * gap + 0.09, approx=True)
                high, low = split(kern)
                value = jnp.dot(high, both, preferred_element_type=F32) + jnp.dot(low, both, preferred_element_type=F32)
                if s == 0:
                    acc[k, at, :] = value
                else:
                    acc[k, at, :] += value

    own[1].wait()
    for d in range(2, ncol, 2):
        lcopies[d].wait_recv()
        lcopies[d + 1].start()
    lcopies[1].wait_recv()
    for d in range(2, ncol, 2):
        lcopies[d + 1].wait_recv()

    sigma[...] = jnp.zeros_like(sigma)
    for d in range(ncol):
        lhigh, llow = split(lbuf[d].T)
        left = jnp.concatenate([lhigh, llow], axis=0)
        at = pl.ds(pl.multiple_of(flip(col, d) * lrows, lrows), lrows)
        for k in range(ne):
            wide = acc[k, at, :]
            high, low = split(wide[:, :ns] + wide[:, ns:])
            top = jnp.dot(left, high, preferred_element_type=F32)
            more = jnp.dot(lhigh, low, preferred_element_type=F32)
            sigma[:, k * ns : (k + 1) * ns] += top[:ns] + top[ns:] + more

    size = part.shape[1]
    for p in range(n):
        part[p] = sigma[p * size : (p + 1) * size, :]

    def peer_of(d):
        peer = lax.rem(me + d, n)
        return peer, (lax.div(peer, ncol), lax.rem(peer, ncol))

    def scatter(d):
        peer, place = peer_of(d)
        return pltpu.make_async_remote_copy(
            part.at[peer], recv.at[d], ssend.at[d], srecv.at[d], device_id=place, device_id_type=MESH)

    def spread(d):
        _, place = peer_of(d)
        return pltpu.make_async_remote_copy(
            gat.at[me], gat.at[me], gsend.at[d], grecv.at[d], device_id=place, device_id_type=MESH)

    @pl.loop(1, n)
    def _(d):
        scatter(d).start()

    recv[0] = part[me]

    @pl.loop(1, n)
    def _(d):
        scatter(d).wait_recv()

    gat[me] = jnp.sum(recv[...], axis=0)

    @pl.loop(1, n)
    def _(d):
        spread(d).start()

    @pl.loop(1, n)
    def _(d):
        spread(d).wait_recv()

    for p in range(n):
        out[p * size : (p + 1) * size, :] = gat[p]

    for copy in rcopies[1:] + lcopies[1:]:
        copy.wait_send()

    @pl.loop(1, n)
    def _(d):
        scatter(d).wait_send()
        spread(d).wait_send()


def fused(nrow, ncol, tile, omega_sq, pole_freq, mtx_left, mtx_right, band_ids, band_energy, eval_energy):
    rows, cols = omega_sq.shape
    lrows, ns = mtx_left.shape[1:]
    rrows = mtx_right.shape[1]
    ne = eval_energy.shape[0]
    n = nrow * ncol
    size = ns // n
    dma = pltpu.SemaphoreType.DMA
    smem = pl.BlockSpec(memory_space=pltpu.SMEM)
    anywhere = pl.BlockSpec(memory_space=pl.ANY)
    return pl.pallas_call(
        functools.partial(body, nrow, ncol, tile),
        out_shape=jax.ShapeDtypeStruct((ns, ne * ns), F32),
        in_specs=[smem] * 3 + [anywhere] * 4,
        out_specs=pl.BlockSpec(memory_space=pltpu.VMEM),
        scratch_shapes=[
            pltpu.VMEM((nrow, rows, rrows), F32),
            pltpu.VMEM((nrow, rows, rrows), F32),
            pltpu.VMEM((nrow, rrows, ns), F32),
            pltpu.VMEM((ncol, lrows, ns), F32),
            pltpu.VMEM((rrows, 2 * ns), BF16),
            pltpu.VMEM((ne, rows, 2 * ns), F32),
            pltpu.VMEM((ns, ne * ns), F32),
            pltpu.VMEM((n, size, ne * ns), F32),
            pltpu.VMEM((n, size, ne * ns), F32),
            pltpu.VMEM((n, size, ne * ns), F32),
            dma((nrow,)), dma((nrow,)), dma((2,)),
            dma((nrow,)), dma((nrow,)), dma((ncol,)), dma((ncol,)),
            dma((n,)), dma((n,)), dma((n,)), dma((n,)),
        ],
        compiler_params=pltpu.CompilerParams(
            collective_id=0, has_side_effects=True, vmem_limit_bytes=48 * 1024 * 1024
        ),
        cost_estimate=pl.CostEstimate(
            flops=6 * rows * cols * ns * ne, bytes_accessed=8 * rows * cols, transcendentals=0
        ),
    )(band_ids, band_energy, eval_energy, omega_sq, pole_freq, mtx_left[0], mtx_right[0])


def shards(nrow, ncol, omega_sq, pole_freq, mtx_left, *rest):
    rows, cols = omega_sq.shape
    lrows, ns = mtx_left.shape[1:]
    n = nrow * ncol
    powers = nrow & (nrow - 1) == 0 and ncol & (ncol - 1) == 0 and ncol > 1
    fits = powers and ns % 128 == 0 and n <= ns and ns % n == 0 and lrows % 128 == 0
    fits = fits and cols % (128 * nrow) == 0 and rows * cols * 8 <= 16 * 1024 * 1024
    if not fits:
        return plain(omega_sq, pole_freq, mtx_left, *rest)
    return fused(nrow, ncol, 128, omega_sq, pole_freq, mtx_left, *rest)


def solution(mesh):
    return jax.shard_map(
        functools.partial(shards, mesh.shape["row"], mesh.shape["col"]),
        mesh=mesh,
        in_specs=(
            P("row", "col"),
            P("row", "col"),
            P(None, ("row", "col"), None),
            P(None, ("col", "row"), None),
            P(),
            P(),
            P(),
        ),
        out_specs=P(),
        check_vma=False,
    )
```

time: 195 us -> 50 us (0.26)
  waiting for transfers between devices: 124 us -> 0 us
  Pallas kernels: 0 us -> 45.4 us
  matrix products: 37.8 us -> 0 us
  between operations: 14.1 us -> 0.67 us
  blocking collectives: 12.8 us -> 0 us
  other arithmetic: 2.55 us -> 0 us
    psum x1 -> x0, waiting for transfers between devices: 123 us -> none  [shards(): return lax.psum(total, ('row', 'col'))]
    pallas_call x0 -> x1, Pallas kernels: none -> 45.4 us  [fused(): pl.pallas_call(functools.partial(body, nrow, ncol, tile), out_shape=jax.S...]
    dot_general x4 -> x0, matrix products: 37.8 us -> none  [the longest x3 30.9 us: kernel_rows(): jnp.dot(kern, right_cols, preferred_element_type=jnp.float32, precision=l...]
    all_gather x1 -> x0, blocking collectives: 12.8 us -> none  [shards(): right_cols = lax.all_gather(mtx_right[0], 'row', axis=0, tiled=True)]
    unnamed x8 -> x9, local copies, waits for them, and re-layouts: 0.02 us -> 3.79 us
  transfers between devices with their start and end apart: 2 -> 0, of which waited for: 1 -> 0; matrix products, arithmetic and copies ran while one was open for 18% -> 0% of each run, Pallas kernels for 0% -> 0%
where the time goes in v1:
time: 50 us; the launch traced here: 49.8 us
  Pallas kernels  45.4 us (91%)
  local copies, waits for them, and re-layouts  3.79 us (8%)
  between operations  0.67 us (1%)
    pallas_call x1, Pallas kernels, fused(): pl.pallas_call(functools.partial(body, nrow, ncol, tile), out_shape=jax.S...  45.4 us
    unnamed x9, local copies, waits for them, and re-layouts  3.79 us

profile of v1, /device:TPU:0, one launch (start us, length us, event | category | flops | bytes accessed | tf_op | source)
XLA Modules:
  0.0 49.8 jit_solution(17425651171378020320)
XLA Ops:
  0.7 0.0 copy-start
  0.7 0.9 %copy-done = f32[1,256,128]{2,1,0:T(8,128)S(1)} copy-done((f32[1,256,128]{2,1,0:T(8,128)S(1)}, f32[1,256,128]{2,1,0:T(8,128)}, u32[]{:S(2)}) %copy-start) | copy-done | bytes 131096
  1.6 0.0 copy-start.1
  1.6 0.9 %copy-done.1 = f32[1,256,128]{2,1,0:T(8,128)S(1)} copy-done((f32[1,256,128]{2,1,0:T(8,128)S(1)}, f32[1,256,128]{2,1,0:T(8,128)}, u32[]{:S(2)}) %copy-start.1) | copy-done | bytes 131096
  2.5 0.0 copy-start.2
  2.5 0.7 %copy-done.2 = f32[64]{0:T(128)S(1)} copy-done((f32[64]{0:T(128)S(1)}, f32[64]{0:T(128)}, u32[]{:S(2)}) %copy-start.2) | copy-done | bytes 280
  3.1 0.0 copy-start.3
  3.1 0.7 %copy-done.3 = f32[3]{0:T(128)S(1)} copy-done((f32[3]{0:T(128)S(1)}, f32[3]{0:T(128)}, u32[]{:S(2)}) %copy-start.3) | copy-done | bytes 36
  3.8 45.4 %shard_map.73 = f32[128,384]{1,0:T(8,128)S(1)} custom-call(s32[1]{0:T(128)S(6)} %copy.9.ids, f32[64]{0:T(128)S(1)} %copy-done.2, f32[3]{0:T(128)S(1)} %copy-done.3, f32[2048,1024]{1,0:T(8,128)} %w_hbm.1, f32[2048,1024]{1,0:T(8,128)} %f_hbm.1, f32[256,128]{1,0:T(8,128)S(1)} %bitcast.2, f32[256,128]{1,0:T(8,128)S(1)} %bitcast.3), custom_call_target="tpu_custom_call" | custom-call | flops 4831838208 | bytes 16777216 | tf_op jit(solution)/shard_map/pallas_call | solution.py:225
  49.2 0.7 %copy.10 = f32[128,384]{1,0:T(8,128)} copy(f32[128,384]{1,0:T(8,128)S(1)} %shard_map.73) | data formatting | bytes 393216
Async XLA Ops:
  0.7 0.9 %copy-start = (f32[1,256,128]{2,1,0:T(8,128)S(1)}, f32[1,256,128]{2,1,0:T(8,128)}, u32[]{:S(2)}) copy-start(f32[1,256,128]{2,1,0:T(8,128)} %param.9) | copy-start | bytes 393220
  1.6 0.9 %copy-start.1 = (f32[1,256,128]{2,1,0:T(8,128)S(1)}, f32[1,256,128]{2,1,0:T(8,128)}, u32[]{:S(2)}) copy-start(f32[1,256,128]{2,1,0:T(8,128)} %param.10) | copy-start | bytes 393220
  2.5 0.7 %copy-start.2 = (f32[64]{0:T(128)S(1)}, f32[64]{0:T(128)}, u32[]{:S(2)}) copy-start(f32[64]{0:T(128)} %levels.1) | copy-start | bytes 772
  3.1 0.7 %copy-start.3 = (f32[3]{0:T(128)S(1)}, f32[3]{0:T(128)}, u32[]{:S(2)}) copy-start(f32[3]{0:T(128)} %evals.1) | copy-start | bytes 40

commit v2 on v1

--- a/solution.py
+++ b/solution.py
@@ -52,16 +52,14 @@
 
 def body(
     nrow, ncol, tile,
-    ids, levels, evals, w_hbm, f_hbm, l_hbm, r_hbm, out,
-    wbuf, fbuf, rbuf, lbuf, rsplit, acc, sigma, part, recv, gat,
-    wsem, fsem, ownsem, rsend, rrecv, lsend, lrecv, ssend, srecv, gsend, grecv,
+    ids_hbm, levels_hbm, evals_hbm, w_hbm, f_hbm, l_hbm, r_hbm, out,
+    ids, levels, evals, wbuf, fbuf, rbuf, lbuf, rsplit, acc, sigma, theirs, mine, bands, pairs, joined, full,
+    wsem, fsem, ownsem, rsend, rrecv, lsend, lrecv, ssend, srecv, gsend, grecv, asend, arecv, bsend, brecv, smallsem,
 ):
     ne = evals.shape[0]
     rows, depth = wbuf.shape[1:]
     lrows, ns = lbuf.shape[1:]
-    n = nrow * ncol
     row, col = lax.axis_index("row"), lax.axis_index("col")
-    me = row * ncol + col
 
     loads = []
     for s in range(nrow):
@@ -76,12 +74,18 @@
         pltpu.make_async_copy(l_hbm, lbuf.at[0], ownsem.at[1]),
     ]
 
+    small = [
+        pltpu.make_async_copy(source, target, smallsem.at[i])
+        for i, (source, target) in enumerate([(ids_hbm, ids), (levels_hbm, levels), (evals_hbm, evals)])
+    ]
+    for copy in small:
+        copy.start()
     barrier = pltpu.get_barrier_semaphore()
 
-    @pl.loop(1, n)
-    def _(d):
-        peer = lax.rem(me + d, n)
-        pl.semaphore_signal(barrier, inc=1, device_id=(lax.div(peer, ncol), lax.rem(peer, ncol)), device_id_type=MESH)
+    for d in range(1, nrow):
+        pl.semaphore_signal(barrier, inc=1, device_id=(flip(row, d), col), device_id_type=MESH)
+    for d in range(1, ncol):
+        pl.semaphore_signal(barrier, inc=1, device_id=(row, flip(col, d)), device_id_type=MESH)
 
     own[0].start()
     for copy in loads[0]:
@@ -90,7 +94,7 @@
     for pair in loads[1:]:
         for copy in pair:
             copy.start()
-    pl.semaphore_wait(barrier, n - 1)
+    pl.semaphore_wait(barrier, nrow + ncol - 2)
 
     rcopies = [None] + [
         pltpu.make_async_remote_copy(
@@ -112,6 +116,8 @@
     for d in range(2, ncol, 2):
         lcopies[d].start()
 
+    for copy in small:
+        copy.wait()
     level = levels[ids[0]]
     shifts = [evals[k] - level for k in range(ne)]
 
@@ -121,8 +127,10 @@
         else:
             rcopies[s].wait_recv()
         high, low = split(rbuf[s])
-        rsplit[:, :ns] = high
-        rsplit[:, ns:] = low
+        rsplit[:depth, :ns] = high
+        rsplit[:depth, ns:] = low
+        rsplit[depth:, :ns] = high
+        rsplit[depth:, ns:] = low
         for copy in loads[s]:
             copy.wait()
 
@@ -136,22 +144,19 @@
                 gap = shifts[k] - freq
                 kern = ratio * gap * pltpu.reciprocal(gap * gap + 0.09, approx=True)
                 high, low = split(kern)
-                value = jnp.dot(high, both, preferred_element_type=F32) + jnp.dot(low, both, preferred_element_type=F32)
+                value = jnp.dot(jnp.concatenate([high, low], axis=1), both, preferred_element_type=F32)
                 if s == 0:
                     acc[k, at, :] = value
                 else:
                     acc[k, at, :] += value
 
     own[1].wait()
-    for d in range(2, ncol, 2):
-        lcopies[d].wait_recv()
-        lcopies[d + 1].start()
-    lcopies[1].wait_recv()
-    for d in range(2, ncol, 2):
-        lcopies[d + 1].wait_recv()
-
     sigma[...] = jnp.zeros_like(sigma)
-    for d in range(ncol):
+    for d in [0, 1, *range(2, ncol, 2), *range(3, ncol, 2)]:
+        if d:
+            lcopies[d].wait_recv()
+            if d % 2 == 0:
+                lcopies[d + 1].start()
         lhigh, llow = split(lbuf[d].T)
         left = jnp.concatenate([lhigh, llow], axis=0)
         at = pl.ds(pl.multiple_of(flip(col, d) * lrows, lrows), lrows)
@@ -162,54 +167,62 @@
             more = jnp.dot(lhigh, low, preferred_element_type=F32)
             sigma[:, k * ns : (k + 1) * ns] += top[:ns] + top[ns:] + more
 
-    size = part.shape[1]
-    for p in range(n):
-        part[p] = sigma[p * size : (p + 1) * size, :]
-
-    def peer_of(d):
-        peer = lax.rem(me + d, n)
-        return peer, (lax.div(peer, ncol), lax.rem(peer, ncol))
-
-    def scatter(d):
-        peer, place = peer_of(d)
+    side, place = lax.rem(col, 2), lax.div(col, 2)
+    half, piece = ns // 2, ns // 2 // nrow
+    npair = ncol // 2
+
+    def half_of(index):
+        return pl.ds(pl.multiple_of(index * half, half), half)
+
+    def piece_of(index):
+        return pl.ds(pl.multiple_of(index * piece, piece), piece)
+
+    def over_row(source, target, s, send, landed):
         return pltpu.make_async_remote_copy(
-            part.at[peer], recv.at[d], ssend.at[d], srecv.at[d], device_id=place, device_id_type=MESH)
-
-    def spread(d):
-        _, place = peer_of(d)
+            source, target, send.at[s], landed.at[s], device_id=(flip(row, s), col), device_id_type=MESH)
+
+    def over_col(source, target, d, send, landed):
         return pltpu.make_async_remote_copy(
-            gat.at[me], gat.at[me], gsend.at[d], grecv.at[d], device_id=place, device_id_type=MESH)
-
-    @pl.loop(1, n)
-    def _(d):
-        scatter(d).start()
-
-    recv[0] = part[me]
-
-    @pl.loop(1, n)
-    def _(d):
-        scatter(d).wait_recv()
-
-    gat[me] = jnp.sum(recv[...], axis=0)
-
-    @pl.loop(1, n)
-    def _(d):
-        spread(d).start()
-
-    @pl.loop(1, n)
-    def _(d):
-        spread(d).wait_recv()
-
-    for p in range(n):
-        out[p * size : (p + 1) * size, :] = gat[p]
-
-    for copy in rcopies[1:] + lcopies[1:]:
+            source, target, send.at[d], landed.at[d], device_id=(row, flip(col, d)), device_id_type=MESH)
+
+    first = over_col(sigma.at[half_of(1 - side)], theirs, 1, ssend, srecv)
+    first.start()
+    first.wait_recv()
+    mine[...] = sigma[half_of(side), :] + theirs[...]
+
+    second = [over_row(mine.at[piece_of(flip(row, s))], bands.at[s], s, asend, arecv) for s in range(1, nrow)]
+    for copy in second:
+        copy.start()
+    total = mine[piece_of(row), :]
+    for s, copy in enumerate(second):
+        copy.wait_recv()
+        total += bands[s + 1]
+    pairs[place] = total
+
+    third = [over_col(pairs.at[place], pairs.at[place], d, gsend, grecv) for d in range(2, ncol, 2)]
+    for copy in third:
+        copy.start()
+    for copy in third:
+        copy.wait_recv()
+    total = pairs[0]
+    for p in range(1, npair):
+        total += pairs[p]
+    joined[piece_of(row), :] = total
+
+    fourth = [over_row(joined.at[piece_of(row)], joined.at[piece_of(row)], s, bsend, brecv) for s in range(1, nrow)]
+    for copy in fourth:
+        copy.start()
+    for copy in fourth:
+        copy.wait_recv()
+
+    fifth = over_col(joined, full, 1, gsend, grecv)
+    fifth.start()
+    out[half_of(side), :] = joined[...]
+    fifth.wait_recv()
+    out[half_of(1 - side), :] = full[...]
+
+    for copy in rcopies[1:] + lcopies[1:] + [first] + second + third + fourth + [fifth]:
         copy.wait_send()
-
-    @pl.loop(1, n)
-    def _(d):
-        scatter(d).wait_send()
-        spread(d).wait_send()
 
 
 def fused(nrow, ncol, tile, omega_sq, pole_freq, mtx_left, mtx_right, band_ids, band_energy, eval_energy):
@@ -217,30 +230,34 @@
     lrows, ns = mtx_left.shape[1:]
     rrows = mtx_right.shape[1]
     ne = eval_energy.shape[0]
-    n = nrow * ncol
-    size = ns // n
     dma = pltpu.SemaphoreType.DMA
-    smem = pl.BlockSpec(memory_space=pltpu.SMEM)
-    anywhere = pl.BlockSpec(memory_space=pl.ANY)
+    hbm = pl.BlockSpec(memory_space=pltpu.HBM)
     return pl.pallas_call(
         functools.partial(body, nrow, ncol, tile),
         out_shape=jax.ShapeDtypeStruct((ns, ne * ns), F32),
-        in_specs=[smem] * 3 + [anywhere] * 4,
+        in_specs=[hbm] * 7,
         out_specs=pl.BlockSpec(memory_space=pltpu.VMEM),
         scratch_shapes=[
+            pltpu.SMEM(band_ids.shape, jnp.int32),
+            pltpu.SMEM(band_energy.shape, F32),
+            pltpu.SMEM(eval_energy.shape, F32),
             pltpu.VMEM((nrow, rows, rrows), F32),
             pltpu.VMEM((nrow, rows, rrows), F32),
             pltpu.VMEM((nrow, rrows, ns), F32),
             pltpu.VMEM((ncol, lrows, ns), F32),
-            pltpu.VMEM((rrows, 2 * ns), BF16),
+            pltpu.VMEM((2 * rrows, 2 * ns), BF16),
             pltpu.VMEM((ne, rows, 2 * ns), F32),
             pltpu.VMEM((ns, ne * ns), F32),
-            pltpu.VMEM((n, size, ne * ns), F32),
-            pltpu.VMEM((n, size, ne * ns), F32),
-            pltpu.VMEM((n, size, ne * ns), F32),
+            pltpu.VMEM((ns // 2, ne * ns), F32),
+            pltpu.VMEM((ns // 2, ne * ns), F32),
+            pltpu.VMEM((nrow, ns // 2 // nrow, ne * ns), F32),
+            pltpu.VMEM((ncol // 2, ns // 2 // nrow, ne * ns), F32),
+            pltpu.VMEM((ns // 2, ne * ns), F32),
+            pltpu.VMEM((ns // 2, ne * ns), F32),
             dma((nrow,)), dma((nrow,)), dma((2,)),
             dma((nrow,)), dma((nrow,)), dma((ncol,)), dma((ncol,)),
-            dma((n,)), dma((n,)), dma((n,)), dma((n,)),
+            dma((ncol,)), dma((ncol,)), dma((ncol,)), dma((ncol,)),
+            dma((nrow,)), dma((nrow,)), dma((nrow,)), dma((nrow,)), dma((3,)),
         ],
         compiler_params=pltpu.CompilerParams(
             collective_id=0, has_side_effects=True, vmem_limit_bytes=48 * 1024 * 1024
@@ -254,13 +271,12 @@
 def shards(nrow, ncol, omega_sq, pole_freq, mtx_left, *rest):
     rows, cols = omega_sq.shape
     lrows, ns = mtx_left.shape[1:]
-    n = nrow * ncol
     powers = nrow & (nrow - 1) == 0 and ncol & (ncol - 1) == 0 and ncol > 1
-    fits = powers and ns % 128 == 0 and n <= ns and ns % n == 0 and lrows % 128 == 0
+    fits = powers and rows % 1024 == 0 and ns % 128 == 0 and ns % (16 * nrow) == 0 and lrows % 128 == 0
     fits = fits and cols % (128 * nrow) == 0 and rows * cols * 8 <= 16 * 1024 * 1024
     if not fits:
         return plain(omega_sq, pole_freq, mtx_left, *rest)
-    return fused(nrow, ncol, 128, omega_sq, pole_freq, mtx_left, *rest)
+    return fused(nrow, ncol, min(1024, rows), omega_sq, pole_freq, mtx_left, *rest)
 
 
 def solution(mesh):

time: 50 us -> 41 us (0.82)
  Pallas kernels: 45.4 us -> 36.4 us
    pallas_call x1, Pallas kernels: 45.4 us -> 36.4 us  [fused(): pl.pallas_call(functools.partial(body, nrow, ncol, tile), out_shape=jax.S...]
where the time goes in v2:
time: 41 us; the launch traced here: 40.8 us
  Pallas kernels  36.4 us (89%)
  local copies, waits for them, and re-layouts  3.79 us (9%)
  between operations  0.67 us (2%)
    pallas_call x1, Pallas kernels, fused(): pl.pallas_call(functools.partial(body, nrow, ncol, tile), out_shape=jax.S...  36.4 us
    unnamed x9, local copies, waits for them, and re-layouts  3.79 us

profile of v2, /device:TPU:0, one launch (start us, length us, event | category | flops | bytes accessed | tf_op | source)
XLA Modules:
  0.0 40.8 jit_solution(16975549028741290434)
XLA Ops:
  0.7 0.0 copy-start
  0.7 0.9 %copy-done = f32[1,256,128]{2,1,0:T(8,128)S(1)} copy-done((f32[1,256,128]{2,1,0:T(8,128)S(1)}, f32[1,256,128]{2,1,0:T(8,128)}, u32[]{:S(2)}) %copy-start) | copy-done | bytes 131096
  1.6 0.0 copy-start.1
  1.6 0.9 %copy-done.1 = f32[1,256,128]{2,1,0:T(8,128)S(1)} copy-done((f32[1,256,128]{2,1,0:T(8,128)S(1)}, f32[1,256,128]{2,1,0:T(8,128)}, u32[]{:S(2)}) %copy-start.1) | copy-done | bytes 131096
  2.5 0.0 copy-start.2
  2.5 0.7 %copy-done.2 = f32[64]{0:T(128)S(1)} copy-done((f32[64]{0:T(128)S(1)}, f32[64]{0:T(128)}, u32[]{:S(2)}) %copy-start.2) | copy-done | bytes 280
  3.1 0.0 copy-start.3
  3.1 0.7 %copy-done.3 = f32[3]{0:T(128)S(1)} copy-done((f32[3]{0:T(128)S(1)}, f32[3]{0:T(128)}, u32[]{:S(2)}) %copy-start.3) | copy-done | bytes 36
  3.8 36.4 %shard_map.73 = f32[128,384]{1,0:T(8,128)S(1)} custom-call(s32[1]{0:T(128)S(6)} %copy.9.ids_hbm, f32[64]{0:T(128)S(1)} %copy-done.2, f32[3]{0:T(128)S(1)} %copy-done.3, f32[2048,1024]{1,0:T(8,128)} %w_hbm.1, f32[2048,1024]{1,0:T(8,128)} %f_hbm.1, f32[256,128]{1,0:T(8,128)S(1)} %bitcast.2, f32[256,128]{1,0:T(8,128)S(1)} %bitcast.3), custom_call_target="tpu_custom_call" | custom-call | flops 4831838208 | bytes 16777216 | tf_op jit(solution)/shard_map/pallas_call | solution.py:235
  40.1 0.7 %copy.10 = f32[128,384]{1,0:T(8,128)} copy(f32[128,384]{1,0:T(8,128)S(1)} %shard_map.73) | data formatting | bytes 393216
Async XLA Ops:
  0.7 0.9 %copy-start = (f32[1,256,128]{2,1,0:T(8,128)S(1)}, f32[1,256,128]{2,1,0:T(8,128)}, u32[]{:S(2)}) copy-start(f32[1,256,128]{2,1,0:T(8,128)} %param.9) | copy-start | bytes 393220
  1.6 0.9 %copy-start.1 = (f32[1,256,128]{2,1,0:T(8,128)S(1)}, f32[1,256,128]{2,1,0:T(8,128)}, u32[]{:S(2)}) copy-start(f32[1,256,128]{2,1,0:T(8,128)} %param.10) | copy-start | bytes 393220
  2.5 0.7 %copy-start.2 = (f32[64]{0:T(128)S(1)}, f32[64]{0:T(128)}, u32[]{:S(2)}) copy-start(f32[64]{0:T(128)} %levels_hbm.1) | copy-start | bytes 772
  3.1 0.7 %copy-start.3 = (f32[3]{0:T(128)S(1)}, f32[3]{0:T(128)}, u32[]{:S(2)}) copy-start(f32[3]{0:T(128)} %evals_hbm.1) | copy-start | bytes 40

commit v3 on v2

--- a/solution.py
+++ b/solution.py
@@ -105,16 +105,24 @@
     ]
     lcopies = [None] * ncol
     for d in range(1, ncol):
-        direct = d == 1 or d % 2 == 0
+        relayed = d > 4 and d % 4 == 2
+        if d == 1 or d % 2 == 0 and not relayed:
+            source, mask = l_hbm, d
+        elif relayed:
+            source, mask = lbuf.at[d - 2], 2
+        else:
+            source, mask = lbuf.at[d - 1], 1
         lcopies[d] = pltpu.make_async_remote_copy(
-            l_hbm if direct else lbuf.at[d - 1], lbuf.at[d], lsend.at[d], lrecv.at[d],
-            device_id=(row, flip(col, d if direct else 1)), device_id_type=MESH,
+            source, lbuf.at[d], lsend.at[d], lrecv.at[d],
+            device_id=(row, flip(col, mask)), device_id_type=MESH,
         )
+    early = [d for d in range(2, ncol, 2) if d == 2 or d % 4 == 0]
+    late = [d for d in range(2, ncol, 2) if d not in early]
     for copy in rcopies[1:]:
         copy.start()
+    for d in early[1:] + early[:1] + []:
+        lcopies[d].start()
     lcopies[1].start()
-    for d in range(2, ncol, 2):
-        lcopies[d].start()
 
     for copy in small:
         copy.wait()
@@ -134,7 +142,7 @@
         for copy in loads[s]:
             copy.wait()
 
-        @pl.loop(0, rows // tile)
+        @pl.loop(0, rows // tile, unroll=True)
         def _(t):
             at = pl.ds(pl.multiple_of(t * tile, tile), tile)
             freq = fbuf[s, at, :]
@@ -150,13 +158,23 @@
                 else:
                     acc[k, at, :] += value
 
+        if s == min(1, nrow - 1):
+            for d in early:
+                lcopies[d].wait_recv()
+                if d + 2 in late:
+                    lcopies[d + 2].start()
+                lcopies[d + 1].start()
+
     own[1].wait()
     sigma[...] = jnp.zeros_like(sigma)
-    for d in [0, 1, *range(2, ncol, 2), *range(3, ncol, 2)]:
-        if d:
+    order = [0, 1, *early, *(d + 1 for d in early), *late, *(d + 1 for d in late)]
+    for d in order:
+        if d == 1 or d in late:
             lcopies[d].wait_recv()
-            if d % 2 == 0:
+            if d in late:
                 lcopies[d + 1].start()
+        elif d % 2:
+            lcopies[d].wait_recv()
         lhigh, llow = split(lbuf[d].T)
         left = jnp.concatenate([lhigh, llow], axis=0)
         at = pl.ds(pl.multiple_of(flip(col, d) * lrows, lrows), lrows)
@@ -276,7 +294,7 @@
     fits = fits and cols % (128 * nrow) == 0 and rows * cols * 8 <= 16 * 1024 * 1024
     if not fits:
         return plain(omega_sq, pole_freq, mtx_left, *rest)
-    return fused(nrow, ncol, min(1024, rows), omega_sq, pole_freq, mtx_left, *rest)
+    return fused(nrow, ncol, min(512, rows), omega_sq, pole_freq, mtx_left, *rest)
 
 
 def solution(mesh):

time: 41 us -> 40.2 us (0.980)
  Pallas kernels: 36.4 us -> 35.5 us
    pallas_call x1, Pallas kernels: 36.4 us -> 35.5 us  [fused(): pl.pallas_call(functools.partial(body, nrow, ncol, tile), out_shape=jax.S...]
where the time goes in v3:
time: 40.2 us; the launch traced here: 40 us
  Pallas kernels  35.5 us (88%)
  local copies, waits for them, and re-layouts  3.79 us (9%)
  between operations  0.67 us (2%)
    pallas_call x1, Pallas kernels, fused(): pl.pallas_call(functools.partial(body, nrow, ncol, tile), out_shape=jax.S...  35.5 us
    unnamed x9, local copies, waits for them, and re-layouts  3.79 us

profile of v3, /device:TPU:0, one launch (start us, length us, event | category | flops | bytes accessed | tf_op | source)
XLA Modules:
  0.0 40.0 jit_solution(12345341560018685305)
XLA Ops:
  0.7 0.0 copy-start
  0.7 0.9 %copy-done = f32[1,256,128]{2,1,0:T(8,128)S(1)} copy-done((f32[1,256,128]{2,1,0:T(8,128)S(1)}, f32[1,256,128]{2,1,0:T(8,128)}, u32[]{:S(2)}) %copy-start) | copy-done | bytes 131096
  1.6 0.0 copy-start.1
  1.6 0.9 %copy-done.1 = f32[1,256,128]{2,1,0:T(8,128)S(1)} copy-done((f32[1,256,128]{2,1,0:T(8,128)S(1)}, f32[1,256,128]{2,1,0:T(8,128)}, u32[]{:S(2)}) %copy-start.1) | copy-done | bytes 131096
  2.5 0.0 copy-start.2
  2.5 0.7 %copy-done.2 = f32[64]{0:T(128)S(1)} copy-done((f32[64]{0:T(128)S(1)}, f32[64]{0:T(128)}, u32[]{:S(2)}) %copy-start.2) | copy-done | bytes 280
  3.1 0.0 copy-start.3
  3.1 0.7 %copy-done.3 = f32[3]{0:T(128)S(1)} copy-done((f32[3]{0:T(128)S(1)}, f32[3]{0:T(128)}, u32[]{:S(2)}) %copy-start.3) | copy-done | bytes 36
  3.8 35.5 %shard_map.73 = f32[128,384]{1,0:T(8,128)S(1)} custom-call(s32[1]{0:T(128)S(6)} %copy.9.ids_hbm, f32[64]{0:T(128)S(1)} %copy-done.2, f32[3]{0:T(128)S(1)} %copy-done.3, f32[2048,1024]{1,0:T(8,128)} %w_hbm.1, f32[2048,1024]{1,0:T(8,128)} %f_hbm.1, f32[256,128]{1,0:T(8,128)S(1)} %bitcast.2, f32[256,128]{1,0:T(8,128)S(1)} %bitcast.3), custom_call_target="tpu_custom_call" | custom-call | flops 4831838208 | bytes 16777216 | tf_op jit(solution)/shard_map/pallas_call | solution.py:253
  39.3 0.7 %copy.10 = f32[128,384]{1,0:T(8,128)} copy(f32[128,384]{1,0:T(8,128)S(1)} %shard_map.73) | data formatting | bytes 393216
Async XLA Ops:
  0.7 0.9 %copy-start = (f32[1,256,128]{2,1,0:T(8,128)S(1)}, f32[1,256,128]{2,1,0:T(8,128)}, u32[]{:S(2)}) copy-start(f32[1,256,128]{2,1,0:T(8,128)} %param.9) | copy-start | bytes 393220
  1.6 0.9 %copy-start.1 = (f32[1,256,128]{2,1,0:T(8,128)S(1)}, f32[1,256,128]{2,1,0:T(8,128)}, u32[]{:S(2)}) copy-start(f32[1,256,128]{2,1,0:T(8,128)} %param.10) | copy-start | bytes 393220
  2.5 0.7 %copy-start.2 = (f32[64]{0:T(128)S(1)}, f32[64]{0:T(128)}, u32[]{:S(2)}) copy-start(f32[64]{0:T(128)} %levels_hbm.1) | copy-start | bytes 772
  3.1 0.7 %copy-start.3 = (f32[3]{0:T(128)S(1)}, f32[3]{0:T(128)}, u32[]{:S(2)}) copy-start(f32[3]{0:T(128)} %evals_hbm.1) | copy-start | bytes 40
